TPU v7x, 32 devices: a whole 2x2x4 slice. The times are simulated.
32 devices in a mesh: group: 8 (over y, x, core), replica: 4 (over z).
Axes of the slice: x: 2, y: 2, z: 4, core: 2. Of those that a mesh axis runs over, the one named last changes fastest.
Arguments:
- tokens: bfloat16 [4, 1024, 960], P('replica', 'group'), may hold values from -6 to 6
- positions: int32 [4, 1024], P('replica', 'group'), may hold values from 0 to 999, as said below
- gain_attn: bfloat16 [2, 960], P(None, 'group'), may hold values from 0.5 to 1.5
- w_query: bfloat16 [2, 960, 960], P(None, 'group'), may hold values from -0.1875 to 0.1875
- w_key: bfloat16 [2, 960, 320], P(None, 'group'), may hold values from -0.1875 to 0.1875
- w_value: bfloat16 [2, 960, 320], P(None, 'group'), may hold values from -0.1875 to 0.1875
- w_out: bfloat16 [2, 960, 960], P(None, 'group'), may hold values from -0.5 to 0.5
- gain_ffn: bfloat16 [2, 960], P(None, 'group'), may hold values from 0.5 to 1.5
- w_gate: bfloat16 [2, 960, 2560], P(None, 'group'), may hold values from -0.1875 to 0.1875
- w_up: bfloat16 [2, 960, 2560], P(None, 'group'), may hold values from -0.1875 to 0.1875
- w_down: bfloat16 [2, 2560, 960], P(None, 'group'), may hold values from -0.125 to 0.125
- cotangent: bfloat16 [4, 1024, 960], P('replica', 'group'), may hold values from -6 to 6
Outputs:
- activations: float32 [4, 2, 1024, 960], P('replica', None, 'group')
- grad_tokens: float32 [4, 1024, 960], P('replica', 'group')
- grad_gain_attn: float32 [2, 960], P(None, 'group')
- grad_w_query: float32 [2, 960, 960], P(None, 'group')
- grad_w_key: float32 [2, 960, 320], P(None, 'group')
- grad_w_value: float32 [2, 960, 320], P(None, 'group')
- grad_w_out: float32 [2, 960, 960], P(None, 'group')
- grad_gain_ffn: float32 [2, 960], P(None, 'group')
- grad_w_gate: float32 [2, 960, 2560], P(None, 'group')
- grad_w_up: float32 [2, 960, 2560], P(None, 'group')
- grad_w_down: float32 [2, 2560, 960], P(None, 'group')
Inputs may be any that keep to these rules, and one draw needn't show every extreme that they name: In each sequence positions are 0 at a document's first token and rise by one per token inside a document; every document except a sequence's last has 100 to 1000 tokens; the first token of every sequence has position 0.
All inputs are finite; a program needn't handle non-finite values.
Results may differ from a plain program's by a relative error of at most 0.02.
Values may be sent and summed in bfloat16 or wider, within the bound.
A program may use at most 320 MiB of HBM per device.

v0:
```python
import jax
import jax.numpy as jnp
from jax import lax
from jax.sharding import PartitionSpec as P

HEADS = 15
KV_HEADS = 5
HEAD_DIM = 64
LAYERS = 2
epsilon = 1e-05
rope_base = 100000.0


def forward_dot(left, right):
    return jnp.dot(left, right, preferred_element_type=jnp.float32)


def over_rows(left, right):
    return lax.dot_general(
        left, right, (((0,), (0,)), ((), ())), preferred_element_type=jnp.float32
    )


def against(left, right):
    return lax.dot_general(
        left, right, (((1,), (1,)), ((), ())), preferred_element_type=jnp.float32
    )


def rope_tables(token_positions):
    half_dim = HEAD_DIM // 2
    frequency = rope_base ** (-2.0 * jnp.arange(half_dim, dtype=jnp.float32) / HEAD_DIM)
    angles = token_positions.astype(jnp.float32)[:, None] * frequency[None, :]
    return (jnp.cos(angles)[:, None, :], jnp.sin(angles)[:, None, :])


def rotate(vectors, cosine, sine_table):
    half_dim = HEAD_DIM // 2
    leading, trailing = (vectors[..., :half_dim], vectors[..., half_dim:])
    return jnp.concatenate(
        [leading * cosine - trailing * sine_table, trailing * cosine + leading * sine_table],
        axis=-1,
    )


def rotate_back(vectors, cosine, sine_table):
    half_dim = HEAD_DIM // 2
    leading, trailing = (vectors[..., :half_dim], vectors[..., half_dim:])
    return jnp.concatenate(
        [leading * cosine + trailing * sine_table, trailing * cosine - leading * sine_table],
        axis=-1,
    )


def norm_forward(stream):
    inverse = lax.rsqrt(jnp.mean(stream * stream, axis=-1, keepdims=True) + epsilon)
    return (inverse, stream * inverse)


def norm_back(grad_unit, unit_value, inverse):
    return inverse * (
        grad_unit - unit_value * jnp.mean(grad_unit * unit_value, axis=-1, keepdims=True)
    )


def masked_scores(grouped, key_all, allowed):
    scores = (
        jnp.einsum("qkgd,skd->kgqs", grouped, key_all, preferred_element_type=jnp.float32) * 0.125
    )
    return jnp.where(allowed[None, None], scores, -1e30)


def layer_forward(stream, gathered, allowed, cosine, sine_table):
    gain_attn, w_query, w_key, w_value, w_out, gain_ffn, w_gate, w_up, w_down = gathered
    row_count = stream.shape[0]
    inverse_attn, unit_attn = norm_forward(stream)
    normed_attn = (unit_attn * gain_attn.astype(jnp.float32)).astype(jnp.bfloat16)
    queries = rotate(
        forward_dot(normed_attn, w_query).reshape(row_count, HEADS, HEAD_DIM), cosine, sine_table
    ).astype(jnp.bfloat16)
    own_keys = rotate(
        forward_dot(normed_attn, w_key).reshape(row_count, KV_HEADS, HEAD_DIM), cosine, sine_table
    ).astype(jnp.bfloat16)
    own_values = (
        forward_dot(normed_attn, w_value)
        .astype(jnp.bfloat16)
        .reshape(row_count, KV_HEADS, HEAD_DIM)
    )
    key_all, value_all = (
        lax.all_gather(own_keys, "group", axis=0, tiled=True),
        lax.all_gather(own_values, "group", axis=0, tiled=True),
    )
    grouped = queries.reshape(row_count, KV_HEADS, HEADS // KV_HEADS, HEAD_DIM)
    scores = masked_scores(grouped, key_all, allowed)
    row_max = jnp.max(scores, axis=-1, keepdims=True)
    exponent = jnp.exp(scores - row_max)
    row_total = jnp.sum(exponent, axis=-1, keepdims=True)
    weights_low = (exponent / row_total).astype(jnp.bfloat16)
    mixed_heads = jnp.einsum(
        "kgqs,skd->qkgd", weights_low, value_all, preferred_element_type=jnp.float32
    )
    mixed_heads = mixed_heads.reshape(row_count, HEADS * HEAD_DIM).astype(jnp.bfloat16)
    after_attn = stream + forward_dot(mixed_heads, w_out)
    inverse_ffn, unit_ffn = norm_forward(after_attn)
    normed_ffn = (unit_ffn * gain_ffn.astype(jnp.float32)).astype(jnp.bfloat16)
    gate_value = forward_dot(normed_ffn, w_gate)
    up_value = forward_dot(normed_ffn, w_up)
    hidden = (jax.nn.silu(gate_value) * up_value).astype(jnp.bfloat16)
    result = after_attn + forward_dot(hidden, w_down)
    saved = (
        unit_attn,
        inverse_attn,
        normed_attn,
        grouped,
        row_max,
        row_total,
        mixed_heads,
        unit_ffn,
        inverse_ffn,
        normed_ffn,
        gate_value,
        up_value,
        hidden,
    )
    return (result, saved, (own_keys, own_values), (key_all, value_all))


def replica_total(shares):
    (
        share_gain_attn,
        share_query,
        share_key,
        share_value,
        share_out,
        share_gain_ffn,
        share_gate,
        share_up,
        share_down,
    ) = shares
    return lax.psum(
        (
            share_gain_attn,
            share_query,
            share_key,
            share_value,
            share_out,
            share_gain_ffn,
            share_gate,
            share_up,
            share_down,
        ),
        "replica",
    )


def owned_columns(matrix, owner, members):
    width = matrix.shape[1] // members
    return lax.dynamic_slice_in_dim(matrix, owner * width, width, 1)


def layer_backward(grad_result, gathered, saved, key_all, value_all, allowed, cosine, sine_table):
    gain_attn, w_query, w_key, w_value, w_out, gain_ffn, w_gate, w_up, w_down = gathered
    (
        unit_attn,
        inverse_attn,
        normed_attn,
        grouped,
        row_max,
        row_total,
        mixed_heads,
        unit_ffn,
        inverse_ffn,
        normed_ffn,
        gate_value,
        up_value,
        hidden,
    ) = saved
    row_count = grad_result.shape[0]
    branch_low = grad_result.astype(jnp.bfloat16)
    grad_hidden = against(branch_low, w_down)
    sigmoid_gate = jax.nn.sigmoid(gate_value)
    grad_up_low = (grad_hidden * gate_value * sigmoid_gate).astype(jnp.bfloat16)
    grad_gate_low = (
        grad_hidden * up_value * sigmoid_gate * (1.0 + gate_value * (1.0 - sigmoid_gate))
    ).astype(jnp.bfloat16)
    grad_normed_ffn = against(grad_gate_low, w_gate) + against(grad_up_low, w_up)
    grad_gain_ffn = jnp.sum(grad_normed_ffn * unit_ffn, axis=0)
    grad_after = grad_result + norm_back(
        grad_normed_ffn * gain_ffn.astype(jnp.float32), unit_ffn, inverse_ffn
    )
    after_low = grad_after.astype(jnp.bfloat16)
    grad_mixed = (
        against(after_low, w_out)
        .astype(jnp.bfloat16)
        .reshape(row_count, KV_HEADS, HEADS // KV_HEADS, HEAD_DIM)
    )
    scores = masked_scores(grouped, key_all, allowed)
    weights_soft = jnp.exp(scores - row_max) / row_total
    grad_weights = jnp.einsum(
        "qkgd,skd->kgqs", grad_mixed, value_all, preferred_element_type=jnp.float32
    )
    grad_value_all = jnp.einsum(
        "kgqs,qkgd->skd",
        weights_soft.astype(jnp.bfloat16),
        grad_mixed,
        preferred_element_type=jnp.float32,
    )
    grad_scores = (
        weights_soft * (grad_weights - jnp.sum(grad_weights * weights_soft, axis=-1, keepdims=True))
    ).astype(jnp.bfloat16)
    grad_queries = (
        jnp.einsum("kgqs,skd->qkgd", grad_scores, key_all, preferred_element_type=jnp.float32)
        * 0.125
    )
    grad_key_all = (
        jnp.einsum("kgqs,qkgd->skd", grad_scores, grouped, preferred_element_type=jnp.float32)
        * 0.125
    )
    grad_keys, grad_values = (
        lax.psum_scatter(grad_key_all, "group", scatter_dimension=0, tiled=True),
        lax.psum_scatter(grad_value_all, "group", scatter_dimension=0, tiled=True),
    )
    query_back = rotate_back(grad_queries.reshape(row_count, HEADS, HEAD_DIM), cosine, sine_table)
    query_back = query_back.reshape(row_count, HEADS * HEAD_DIM).astype(jnp.bfloat16)
    key_back = (
        rotate_back(grad_keys, cosine, sine_table)
        .reshape(row_count, KV_HEADS * HEAD_DIM)
        .astype(jnp.bfloat16)
    )
    value_back = grad_values.reshape(row_count, KV_HEADS * HEAD_DIM).astype(jnp.bfloat16)
    grad_normed_attn = (
        against(query_back, w_query) + against(key_back, w_key) + against(value_back, w_value)
    )
    grad_gain_attn = jnp.sum(grad_normed_attn * unit_attn, axis=0)
    grad_stream = grad_after + norm_back(
        grad_normed_attn * gain_attn.astype(jnp.float32), unit_attn, inverse_attn
    )
    owner = lax.axis_index("group")
    members = lax.axis_size("group")
    piece_attn = lax.all_gather(normed_attn, "group", axis=0, tiled=True)
    piece_query = lax.all_gather(query_back, "group", axis=0, tiled=True)
    piece_key = lax.all_gather(key_back, "group", axis=0, tiled=True)
    piece_value = lax.all_gather(value_back, "group", axis=0, tiled=True)
    piece_mixed = lax.all_gather(mixed_heads, "group", axis=0, tiled=True)
    piece_after = lax.all_gather(after_low, "group", axis=0, tiled=True)
    piece_ffn = lax.all_gather(normed_ffn, "group", axis=0, tiled=True)
    piece_gate = lax.all_gather(grad_gate_low, "group", axis=0, tiled=True)
    piece_up = lax.all_gather(grad_up_low, "group", axis=0, tiled=True)
    piece_hidden = lax.all_gather(hidden, "group", axis=0, tiled=True)
    piece_branch = lax.all_gather(branch_low, "group", axis=0, tiled=True)
    left_attn = owned_columns(piece_attn, owner, members)
    left_mixed = owned_columns(piece_mixed, owner, members)
    left_ffn = owned_columns(piece_ffn, owner, members)
    left_hidden = owned_columns(piece_hidden, owner, members)
    gain_shares = (
        lax.psum_scatter(grad_gain_attn, "group", scatter_dimension=0, tiled=True),
        lax.psum_scatter(grad_gain_ffn, "group", scatter_dimension=0, tiled=True),
    )
    shares = (
        gain_shares[0],
        over_rows(left_attn, piece_query),
        over_rows(left_attn, piece_key),
        over_rows(left_attn, piece_value),
        over_rows(left_mixed, piece_after),
        gain_shares[1],
        over_rows(left_ffn, piece_gate),
        over_rows(left_ffn, piece_up),
        over_rows(left_hidden, piece_branch),
    )
    return (grad_stream, shares)


def on_device(
    tokens,
    positions,
    gain_attn,
    w_query,
    w_key,
    w_value,
    w_out,
    gain_ffn,
    w_gate,
    w_up,
    w_down,
    cotangent,
):
    row_count = tokens.shape[1]
    length_all = row_count * lax.axis_size("group")
    row_index = lax.axis_index("group") * row_count + jnp.arange(row_count, dtype=jnp.int32)
    token_positions = positions[0]
    key_index = jnp.arange(length_all, dtype=jnp.int32)
    allowed = (key_index[None, :] <= row_index[:, None]) & (
        key_index[None, :] >= (row_index - token_positions)[:, None]
    )
    cosine, sine_table = rope_tables(token_positions)
    stream = tokens[0].astype(jnp.float32)
    saved_all = []
    own_all = []
    full_all = []
    gathered_all = []
    outputs = []
    for layer_index in range(LAYERS):
        gathered = (
            lax.all_gather(gain_attn[layer_index], "group", axis=0, tiled=True),
            lax.all_gather(w_query[layer_index], "group", axis=0, tiled=True),
            lax.all_gather(w_key[layer_index], "group", axis=0, tiled=True),
            lax.all_gather(w_value[layer_index], "group", axis=0, tiled=True),
            lax.all_gather(w_out[layer_index], "group", axis=0, tiled=True),
            lax.all_gather(gain_ffn[layer_index], "group", axis=0, tiled=True),
            lax.all_gather(w_gate[layer_index], "group", axis=0, tiled=True),
            lax.all_gather(w_up[layer_index], "group", axis=0, tiled=True),
            lax.all_gather(w_down[layer_index], "group", axis=0, tiled=True),
        )
        stream, saved, own_pair, full_pair = layer_forward(
            stream, gathered, allowed, cosine, sine_table
        )
        saved_all.append(saved)
        own_all.append(own_pair)
        full_all.append(full_pair)
        gathered_all.append(gathered)
        outputs.append(stream)
    grad_stream = cotangent[0].astype(jnp.float32)
    owned = [None] * LAYERS
    for layer_index in reversed(range(LAYERS)):
        gathered = (
            lax.all_gather(gain_attn[layer_index], "group", axis=0, tiled=True),
            lax.all_gather(w_query[layer_index], "group", axis=0, tiled=True),
            lax.all_gather(w_key[layer_index], "group", axis=0, tiled=True),
            lax.all_gather(w_value[layer_index], "group", axis=0, tiled=True),
            lax.all_gather(w_out[layer_index], "group", axis=0, tiled=True),
            lax.all_gather(gain_ffn[layer_index], "group", axis=0, tiled=True),
            lax.all_gather(w_gate[layer_index], "group", axis=0, tiled=True),
            lax.all_gather(w_up[layer_index], "group", axis=0, tiled=True),
            lax.all_gather(w_down[layer_index], "group", axis=0, tiled=True),
        )
        key_all, value_all = (
            lax.all_gather(own_all[layer_index][0], "group", axis=0, tiled=True),
            lax.all_gather(own_all[layer_index][1], "group", axis=0, tiled=True),
        )
        grad_stream, shares = layer_backward(
            grad_stream,
            gathered,
            saved_all[layer_index],
            key_all,
            value_all,
            allowed,
            cosine,
            sine_table,
        )
        owned[layer_index] = replica_total(shares)
    stacked = tuple(
        (
            jnp.stack([owned[layer_index][member] for layer_index in range(LAYERS)])
            for member in range(9)
        )
    )
    activations = jnp.stack(outputs)[None]
    return (
        activations,
        grad_stream[None],
        stacked[0],
        stacked[1],
        stacked[2],
        stacked[3],
        stacked[4],
        stacked[5],
        stacked[6],
        stacked[7],
        stacked[8],
    )


def solution(mesh):
    in_specs = (
        P("replica", "group", None),
        P("replica", "group"),
        P(None, "group"),
        P(None, "group", None),
        P(None, "group", None),
        P(None, "group", None),
        P(None, "group", None),
        P(None, "group"),
        P(None, "group", None),
        P(None, "group", None),
        P(None, "group", None),
        P("replica", "group", None),
    )
    out_specs = (
        P("replica", None, "group", None),
        P("replica", "group", None),
        P(None, "group"),
        P(None, "group", None),
        P(None, "group", None),
        P(None, "group", None),
        P(None, "group", None),
        P(None, "group"),
        P(None, "group", None),
        P(None, "group", None),
        P(None, "group", None),
    )
    return jax.shard_map(
        on_device, mesh=mesh, in_specs=in_specs, out_specs=out_specs, check_vma=False
    )
```

profile of v0, /device:TPU:0, one launch (start us, length us, event | category | flops | bytes accessed | tf_op | source)
XLA Modules:
  0.0 1593.5 jit_solution(1129092299961670674)
XLA Ops:
  21.1 15.6 all-reduce.11
  37.8 12.0 all-gather.2
  53.1 10.6 all_gather.158
  64.5 13.1 all-gather.1
  80.3 13.3 all_gather.156
  95.9 20.1 %all-gather.11 = bf16[1,960,320]{2,0,1:T(2,128)(2,1)S(1)} all-gather(bf16[1,120,320]{2,0,1:T(2,128)(2,1)S(1)} %copy.82), channel_id=13, replica_groups=mesh['group'=8,'replica'=4] {'group'}, dimensions={1}, use_global_device_ids=true | all-gather | bytes 691200 | tf_op jit(solution)/shard_map/all_gather | solution.py:306
  119.7 12.5 all-gather.10
  166.6 38.7 %all-gather.90.cloned.1.call-done = bf16[1,2560,960]{2,1,0:T(8,128)(2,1)} async-done(((bf16[1,320,960]{2,1,0:T(8,128)(2,1)}), bf16[1,2560,960]{2,1,0:T(8,128)(2,1)}) %all-gather.90.cloned.1.call-update) | async-done | bytes 4915216 | tf_op jit(solution)/shard_map/all_gather | solution.py:312
  211.4 12.2 all_gather.169
  224.0 14.7 all_gather.167
  241.4 6.9 fusion.241
  252.6 16.1 %all-gather.94.cloned.1.call-done = bf16[1,960,960]{2,1,0:T(8,128)(2,1)} async-done(((bf16[1,120,960]{2,1,0:T(8,128)(2,1)}), bf16[1,960,960]{2,1,0:T(8,128)(2,1)}) %all-gather.94.cloned.1.call-update) | async-done | bytes 1843216 | tf_op jit(solution)/shard_map/all_gather | solution.py:308
  271.7 39.3 %all-gather.98.cloned.1.call-done = bf16[1,960,2560]{2,1,0:T(8,128)(2,1)} async-done(((bf16[1,120,2560]{2,1,0:T(8,128)(2,1)}), bf16[1,960,2560]{2,1,0:T(8,128)(2,1)}) %all-gather.98.cloned.1.call-update) | async-done | bytes 4915216 | tf_op jit(solution)/shard_map/all_gather | solution.py:311
  315.3 39.3 %all-gather.100.cloned.1.call-done = bf16[1,2560,960]{2,1,0:T(8,128)(2,1)} async-done(((bf16[1,320,960]{2,1,0:T(8,128)(2,1)}), bf16[1,2560,960]{2,1,0:T(8,128)(2,1)}) %all-gather.100.cloned.1.call-update) | async-done | bytes 4915216 | tf_op jit(solution)/shard_map/all_gather | solution.py:312
  360.0 36.1 %all-gather.96.cloned.1.call-done = bf16[1,960,2560]{2,1,0:T(8,128)(2,1)} async-done(((bf16[1,120,2560]{2,1,0:T(8,128)(2,1)}), bf16[1,960,2560]{2,1,0:T(8,128)(2,1)}) %all-gather.96.cloned.1.call-update) | async-done | bytes 4915216 | tf_op jit(solution)/shard_map/all_gather | solution.py:310
  396.1 5.8 multiply_convert_fusion.3
  415.0 7.7 fusion.5
  422.7 6.9 fusion.7
  446.0 25.5 %reduce-scatter.5.cloned.1.call-done = f32[128,5,64]{0,2,1:T(8,128)} async-done(((f32[1024,5,64]{0,2,1:T(8,128)}), f32[128,5,64]{0,2,1:T(8,128)}) %reduce-scatter.5.cloned.1.call-update) | async-done | bytes 163856 | tf_op jit(solution)/shard_map/reduce_scatter | solution.py:220
  474.8 37.7 %reduce-scatter.7.cloned.1.call-done = f32[128,5,64]{0,2,1:T(8,128)} async-done(((f32[1024,5,64]{0,2,1:T(8,128)}), f32[128,5,64]{0,2,1:T(8,128)}) %reduce-scatter.7.cloned.1.call-update) | async-done | bytes 163856 | tf_op jit(solution)/shard_map/reduce_scatter | solution.py:221
  519.0 6.5 multiply_convert_fusion.1
  538.8 5.9 fusion.68
  544.7 7.7 fusion.2
  552.4 6.8 fusion.4
  576.6 11.5 all_gather.181
  588.1 12.7 all_gather.183
  608.2 25.1 %all-gather.60.cloned.1.call-done = bf16[1024,960]{0,1:T(8,128)(2,1)} async-done(((bf16[128,960]{0,1:T(8,128)(2,1)}), bf16[1024,960]{0,1:T(8,128)(2,1)}) %all-gather.60.cloned.1.call-update) | async-done | bytes 1966096 | tf_op jit(solution)/shard_map/all_gather | solution.py:244
  636.5 37.8 %reduce-scatter.11.cloned.1.call-done = f32[128,5,64]{0,2,1:T(8,128)} async-done(((f32[1024,5,64]{0,2,1:T(8,128)}), f32[128,5,64]{0,2,1:T(8,128)}) %reduce-scatter.11.cloned.1.call-update) | async-done | bytes 163856 | tf_op jit(solution)/shard_map/reduce_scatter | solution.py:221
  675.2 40.1 %reduce-scatter.9.cloned.1.call-done = f32[128,5,64]{0,2,1:T(8,128)} async-done(((f32[1024,5,64]{0,2,1:T(8,128)}), f32[128,5,64]{0,2,1:T(8,128)}) %reduce-scatter.9.cloned.1.call-update) | async-done | bytes 163856 | tf_op jit(solution)/shard_map/reduce_scatter | solution.py:220
  716.3 11.2 all_gather.180
  727.5 9.6 all_gather.182
  737.1 7.8 all-gather.48.cloned.1.call-done
  749.0 25.8 %all-gather.50.cloned.1.call-done = bf16[1024,960]{0,1:T(8,128)(2,1)} async-done(((bf16[128,960]{0,1:T(8,128)(2,1)}), bf16[1024,960]{0,1:T(8,128)(2,1)}) %all-gather.50.cloned.1.call-update) | async-done | bytes 1966096 | tf_op jit(solution)/shard_map/all_gather | solution.py:241
  778.0 26.3 %all-gather.56.cloned.1.call-done = bf16[1024,960]{0,1:T(8,128)(2,1)} async-done(((bf16[128,960]{0,1:T(8,128)(2,1)}), bf16[1024,960]{0,1:T(8,128)(2,1)}) %all-gather.56.cloned.1.call-update) | async-done | bytes 1966096 | tf_op jit(solution)/shard_map/all_gather | solution.py:244
  804.3 30.1 %all-gather.58.cloned.1.call-done = bf16[1024,960]{0,1:T(8,128)(2,1)} async-done(((bf16[128,960]{0,1:T(8,128)(2,1)}), bf16[1024,960]{0,1:T(8,128)(2,1)}) %all-gather.58.cloned.1.call-update) | async-done | bytes 1966096 | tf_op jit(solution)/shard_map/all_gather | solution.py:245
  837.7 26.2 %all-gather.78.cloned.1.call-done = bf16[1024,960]{0,1:T(8,128)(2,1)} async-done(((bf16[128,960]{0,1:T(8,128)(2,1)}), bf16[1024,960]{0,1:T(8,128)(2,1)}) %all-gather.78.cloned.1.call-update) | async-done | bytes 1966096 | tf_op jit(solution)/shard_map/all_gather | solution.py:250
  864.0 42.9 %all-gather.76.cloned.1.call-done = bf16[1024,2560]{1,0:T(8,128)(2,1)} async-done(((bf16[128,2560]{1,0:T(8,128)(2,1)}), bf16[1024,2560]{1,0:T(8,128)(2,1)}) %all-gather.76.cloned.1.call-update) | async-done | bytes 5242896 | tf_op jit(solution)/shard_map/all_gather | solution.py:249
  911.2 25.2 %all-gather.102.cloned.1.call-done = bf16[1,1024,960]{1,2,0:T(8,128)(2,1)} async-done(((bf16[1,128,960]{1,2,0:T(8,128)(2,1)}), bf16[1,1024,960]{1,2,0:T(8,128)(2,1)}) %all-gather.102.cloned.1.call-update) | async-done | bytes 1966096 | tf_op jit(solution)/shard_map/all_gather | solution.py:250
  936.4 43.5 %all-gather.80.cloned.1.call-done = bf16[1024,2560]{1,0:T(8,128)(2,1)} async-done(((bf16[128,2560]{1,0:T(8,128)(2,1)}), bf16[1024,2560]{1,0:T(8,128)(2,1)}) %all-gather.80.cloned.1.call-update) | async-done | bytes 5242896 | tf_op jit(solution)/shard_map/all_gather | solution.py:249
  984.2 25.1 %all-gather.68.cloned.1.call-done = bf16[1024,960]{0,1:T(8,128)(2,1)} async-done(((bf16[128,960]{0,1:T(8,128)(2,1)}), bf16[1024,960]{0,1:T(8,128)(2,1)}) %all-gather.68.cloned.1.call-update) | async-done | bytes 1966096 | tf_op jit(solution)/shard_map/all_gather | solution.py:246
  1009.2 43.6 %all-gather.74.cloned.1.call-done = bf16[1024,2560]{1,0:T(8,128)(2,1)} async-done(((bf16[128,2560]{1,0:T(8,128)(2,1)}), bf16[1024,2560]{1,0:T(8,128)(2,1)}) %all-gather.74.cloned.1.call-update) | async-done | bytes 5242896 | tf_op jit(solution)/shard_map/all_gather | solution.py:248
  1057.3 39.1 %all-gather.70.cloned.1.call-done = bf16[1024,2560]{1,0:T(8,128)(2,1)} async-done(((bf16[128,2560]{1,0:T(8,128)(2,1)}), bf16[1024,2560]{1,0:T(8,128)(2,1)}) %all-gather.70.cloned.1.call-update) | async-done | bytes 5242896 | tf_op jit(solution)/shard_map/all_gather | solution.py:247
  1101.0 24.9 %all-gather.64.cloned.1.call-done = bf16[1024,960]{0,1:T(8,128)(2,1)} async-done(((bf16[128,960]{0,1:T(8,128)(2,1)}), bf16[1024,960]{0,1:T(8,128)(2,1)}) %all-gather.64.cloned.1.call-update) | async-done | bytes 1966096 | tf_op jit(solution)/shard_map/all_gather | solution.py:246
  1125.8 43.0 %all-gather.72.cloned.1.call-done = bf16[1024,2560]{1,0:T(8,128)(2,1)} async-done(((bf16[128,2560]{1,0:T(8,128)(2,1)}), bf16[1024,2560]{1,0:T(8,128)(2,1)}) %all-gather.72.cloned.1.call-update) | async-done | bytes 5242896 | tf_op jit(solution)/shard_map/all_gather | solution.py:248
  1173.5 38.4 %all-gather.66.cloned.1.call-done = bf16[1024,2560]{1,0:T(8,128)(2,1)} async-done(((bf16[128,2560]{1,0:T(8,128)(2,1)}), bf16[1024,2560]{1,0:T(8,128)(2,1)}) %all-gather.66.cloned.1.call-update) | async-done | bytes 5242896 | tf_op jit(solution)/shard_map/all_gather | solution.py:247
  1225.3 24.6 %all-reduce.8 = (f32[960]{0:T(1024)S(1)}, f32[960]{0:T(1024)S(1)}, f32[960]{0:T(1024)S(1)}, f32[960]{0:T(1024)S(1)}) all-reduce(f32[960]{0:T(1024)S(1)} %copy-done.74, f32[960]{0:T(1024)S(1)} %get-tuple-element.17, f32[960]{0:T(1024)S(1)} %copy-done.73, f32[960]{0:T(1024)S(1)} %copy-done.75), channel_id=26, replica_groups=mesh['group'=8,'replica'=4] {'group'}, use_global_device_ids=true, to_apply=%region_22.23.clone | all-reduce | flops 3840 | bytes 30720
  1250.2 11.6 all-reduce.9
  1264.0 311.0 %all-reduce.14.cloned.1.call-done = (f32[1,120,960]{2,1,0:T(8,128)}, f32[1,120,960]{2,1,0:T(8,128)}, f32[1,120,320]{1,2,0:T(8,128)}, f32[1,120,320]{1,2,0:T(8,12...) async-done(((f32[1,120,960]{2,1,0:T(8,128)}, ...) | async-done | bytes 9830416 | tf_op jit(solution)/shard_map/psum | solution.py:140
  (397 shorter events, 228.2 us)
Async XLA Ops:
  7.2 129.2 %all-gather.82.cloned.1.call-start = ((), (), s32[]{:S(2)}) async-start(), calls=%async_computation.25 | async-start | bytes 2211840 | tf_op jit(solution)/shard_map/all_gather | solution.py:305
  9.2 143.5 %all-gather.84.cloned.1.call-start = ((), (), s32[]{:S(2)}) async-start(), calls=%async_computation.26 | async-start | bytes 2211840 | tf_op jit(solution)/shard_map/all_gather | solution.py:308
  11.3 144.2 %all-gather.86.cloned.1.call-start = ((), (), s32[]{:S(2)}) async-start(), calls=%async_computation.27 | async-start | bytes 5529600 | tf_op jit(solution)/shard_map/all_gather | solution.py:310
  12.5 149.3 %all-gather.88.cloned.1.call-start = ((), (), s32[]{:S(2)}) async-start(), calls=%async_computation.28 | async-start | bytes 5529600 | tf_op jit(solution)/shard_map/all_gather | solution.py:311
  13.7 191.5 %all-gather.90.cloned.1.call-start = ((), (), s32[]{:S(2)}) async-start(), calls=%async_computation.29 | async-start | bytes 5898240 | tf_op jit(solution)/shard_map/all_gather | solution.py:312
  15.4 21.4 %copy-start.2 = (bf16[1,128,960]{1,2,0:T(8,128)(2,1)S(1)}, bf16[1,128,960]{1,2,0:T(8,128)(2,1)}, u32[]{:S(2)}) copy-start(bf16[1,128,960]{1,2,0:T(8,128)(2,1)} %param.12) | copy-start | bytes 737284
  15.4 21.5 %copy-start.59 = (bf16[2,120,320]{1,2,0:T(8,128)(2,1)S(1)}, bf16[2,120,320]{1,2,0:T(8,128)(2,1)}, u32[]{:S(2)}) copy-start(bf16[2,120,320]{1,2,0:T(8,128)(2,1)} %param.16) | copy-start | bytes 460804
  15.4 223.4 %all-gather.92.cloned.1.call-start = ((), (), s32[]{:S(2)}) async-start(), calls=%async_computation.30 | async-start | bytes 2211840 | tf_op jit(solution)/shard_map/all_gather | solution.py:305
  16.0 252.7 %all-gather.94.cloned.1.call-start = ((), (), s32[]{:S(2)}) async-start(), calls=%async_computation.31 | async-start | bytes 2211840 | tf_op jit(solution)/shard_map/all_gather | solution.py:308
  16.7 294.2 %all-gather.98.cloned.1.call-start = ((), (), s32[]{:S(2)}) async-start(), calls=%async_computation.33 | async-start | bytes 5529600 | tf_op jit(solution)/shard_map/all_gather | solution.py:311
  17.5 337.1 %all-gather.100.cloned.1.call-start = ((), (), s32[]{:S(2)}) async-start(), calls=%async_computation.34 | async-start | bytes 5898240 | tf_op jit(solution)/shard_map/all_gather | solution.py:312
  18.2 377.9 %all-gather.96.cloned.1.call-start = ((), (), s32[]{:S(2)}) async-start(), calls=%async_computation.32 | async-start | bytes 5529600 | tf_op jit(solution)/shard_map/all_gather | solution.py:310
  18.8 452.7 %reduce-scatter.5.cloned.1.call-start = ((), (), s32[]{:S(2)}) async-start(), calls=%async_computation.4 | async-start | bytes 1474560 | tf_op jit(solution)/shard_map/reduce_scatter | solution.py:220
  36.7 103.5 %copy-start.61 = (f32[960]{0:T(1024)}, f32[960]{0:T(1024)S(1)}, u32[]{:S(2)}) copy-start(f32[960]{0:T(1024)S(1)} %convert_element_type.211) | copy-start | bytes 11524
  36.9 103.3 %copy-start.76 = (f32[128]{0:T(128)}, f32[128]{0:T(128)S(1)}, u32[]{:S(2)}) copy-start(f32[128]{0:T(128)S(1)} %add_rsqrt_fusion.3) | copy-start | bytes 1540
  52.2 25.5 %copy-start.7 = (bf16[1,960,320]{1,2,0:T(8,128)(2,1)}, bf16[1,960,320]{1,2,0:T(8,128)(2,1)S(1)}, u32[]{:S(2)}) copy-start(bf16[1,960,320]{1,2,0:T(8,128)(2,1)S(1)} %copy.49) | copy-start | bytes 1843204
  52.4 27.6 %copy-start.18 = (bf16[128,960]{0,1:T(8,128)(2,1)}, bf16[128,960]{0,1:T(8,128)(2,1)S(1)}, u32[]{:S(2)}) copy-start(bf16[128,960]{0,1:T(8,128)(2,1)S(1)} %fusion.169) | copy-start | bytes 737284
  94.8 24.7 %copy-start.53 = (bf16[1,120,320]{1,2,0:T(8,128)(2,1)S(1)}, bf16[1,120,320]{1,2,0:T(8,128)(2,1)}, u32[]{:S(2)}) copy-start(bf16[1,120,320]{1,2,0:T(8,128)(2,1)} %get-tuple-element.82) | copy-start | bytes 230404
  166.6 42.9 %copy-start.5 = (bf16[128,2560]{1,0:T(8,128)(2,1)}, bf16[128,2560]{1,0:T(8,128)(2,1)S(1)}, u32[]{:S(2)}) copy-start(bf16[128,2560]{1,0:T(8,128)(2,1)S(1)} %get-tuple-element.96) | copy-start | bytes 1966084
  209.7 29.2 %copy-start.4 = (bf16[128,960]{0,1:T(8,128)(2,1)}, bf16[128,960]{0,1:T(8,128)(2,1)S(1)}, u32[]{:S(2)}) copy-start(bf16[128,960]{0,1:T(8,128)(2,1)S(1)} %multiply_convert_fusion.7) | copy-start | bytes 737284
  252.6 18.6 %copy-start.33 = (bf16[5,64,3,128]{3,1,2,0:T(8,128)(2,1)}, bf16[5,64,3,128]{3,1,2,0:T(8,128)(2,1)S(1)}, u32[]{:S(2)}) copy-start(bf16[5,64,3,128]{3,1,2,0:T(8,128)(2,1)S(1)} %fusion.117) | copy-start | bytes 737284
  252.6 18.6 %copy-start.65 = (f32[960]{0:T(1024)S(1)}, f32[960]{0:T(1024)}, u32[]{:S(2)}) copy-start(f32[960]{0:T(1024)} %convert_element_type.214) | copy-start | bytes 11524
  271.4 124.7 %copy-start.19 = (bf16[128,960]{0,1:T(8,128)(2,1)}, bf16[128,960]{0,1:T(8,128)(2,1)S(1)}, u32[]{:S(2)}) copy-start(bf16[128,960]{0,1:T(8,128)(2,1)S(1)} %multiply_convert_fusion.6) | copy-start | bytes 737284
  271.7 82.9 %copy-start.12 = (bf16[1,128,960]{1,2,0:T(8,128)(2,1)S(1)}, bf16[1,128,960]{1,2,0:T(8,128)(2,1)}, u32[]{:S(2)}) copy-start(bf16[1,128,960]{1,2,0:T(8,128)(2,1)} %param.23) | copy-start | bytes 737284
  434.0 78.5 %reduce-scatter.7.cloned.1.call-start = ((), (), s32[]{:S(2)}) async-start(), calls=%async_computation.5 | async-start | bytes 1474560 | tf_op jit(solution)/shard_map/reduce_scatter | solution.py:221
  439.8 161.0 %all-gather.52.cloned.1.call-start = ((), (), s32[]{:S(2)}) async-start(), calls=%async_computation.10 | async-start | bytes 2211840 | tf_op jit(solution)/shard_map/all_gather | solution.py:240
  440.5 164.4 %all-gather.54.cloned.1.call-start = ((), (), s32[]{:S(2)}) async-start(), calls=%async_computation.11 | async-start | bytes 2211840 | tf_op jit(solution)/shard_map/all_gather | solution.py:241
  444.6 163.5 %all-gather.62.cloned.1.call-start = ((), (), s32[]{:S(2)}) async-start(), calls=%async_computation.15 | async-start | bytes 2211840 | tf_op jit(solution)/shard_map/all_gather | solution.py:245
  445.2 188.1 %all-gather.60.cloned.1.call-start = ((), (), s32[]{:S(2)}) async-start(), calls=%async_computation.14 | async-start | bytes 2211840 | tf_op jit(solution)/shard_map/all_gather | solution.py:244
  445.8 228.5 %reduce-scatter.11.cloned.1.call-start = ((), (), s32[]{:S(2)}) async-start(), calls=%async_computation.7 | async-start | bytes 1474560 | tf_op jit(solution)/shard_map/reduce_scatter | solution.py:221
  472.5 41.0 %copy-start.34 = (bf16[128,5,64]{0,2,1:T(8,128)(2,1)}, bf16[128,5,64]{0,2,1:T(8,128)(2,1)S(1)}, u32[]{:S(2)}) copy-start(bf16[128,5,64]{0,2,1:T(8,128)(2,1)S(1)} %pad_maximum_fusion.13) | copy-start | bytes 245764
  544.6 170.7 %reduce-scatter.9.cloned.1.call-start = ((), (), s32[]{:S(2)}) async-start(), calls=%async_computation.6 | async-start | bytes 1474560 | tf_op jit(solution)/shard_map/reduce_scatter | solution.py:220
  563.6 181.3 %all-gather.48.cloned.1.call-start = ((), (), s32[]{:S(2)}) async-start(), calls=%async_computation.8 | async-start | bytes 2211840 | tf_op jit(solution)/shard_map/all_gather | solution.py:240
  564.3 210.5 %all-gather.50.cloned.1.call-start = ((), (), s32[]{:S(2)}) async-start(), calls=%async_computation.9 | async-start | bytes 2211840 | tf_op jit(solution)/shard_map/all_gather | solution.py:241
  568.3 236.0 %all-gather.56.cloned.1.call-start = ((), (), s32[]{:S(2)}) async-start(), calls=%async_computation.12 | async-start | bytes 2211840 | tf_op jit(solution)/shard_map/all_gather | solution.py:244
  569.0 265.4 %all-gather.58.cloned.1.call-start = ((), (), s32[]{:S(2)}) async-start(), calls=%async_computation.13 | async-start | bytes 2211840 | tf_op jit(solution)/shard_map/all_gather | solution.py:245
  569.8 294.2 %all-gather.78.cloned.1.call-start = ((), (), s32[]{:S(2)}) async-start(), calls=%async_computation.23 | async-start | bytes 2211840 | tf_op jit(solution)/shard_map/all_gather | solution.py:250
  570.5 336.3 %all-gather.76.cloned.1.call-start = ((), (), s32[]{:S(2)}) async-start(), calls=%async_computation.22 | async-start | bytes 5898240 | tf_op jit(solution)/shard_map/all_gather | solution.py:249
  571.1 365.3 %all-gather.102.cloned.1.call-start = ((), (), s32[]{:S(2)}) async-start(), calls=%async_computation.35 | async-start | bytes 2211840 | tf_op jit(solution)/shard_map/all_gather | solution.py:250
  571.9 408.0 %all-gather.80.cloned.1.call-start = ((), (), s32[]{:S(2)}) async-start(), calls=%async_computation.24 | async-start | bytes 5898240 | tf_op jit(solution)/shard_map/all_gather | solution.py:249
  572.4 436.8 %all-gather.68.cloned.1.call-start = ((), (), s32[]{:S(2)}) async-start(), calls=%async_computation.18 | async-start | bytes 2211840 | tf_op jit(solution)/shard_map/all_gather | solution.py:246
  573.0 479.8 %all-gather.74.cloned.1.call-start = ((), (), s32[]{:S(2)}) async-start(), calls=%async_computation.21 | async-start | bytes 5898240 | tf_op jit(solution)/shard_map/all_gather | solution.py:248
  573.8 522.7 %all-gather.70.cloned.1.call-start = ((), (), s32[]{:S(2)}) async-start(), calls=%async_computation.19 | async-start | bytes 5898240 | tf_op jit(solution)/shard_map/all_gather | solution.py:247
  574.5 551.3 %all-gather.64.cloned.1.call-start = ((), (), s32[]{:S(2)}) async-start(), calls=%async_computation.16 | async-start | bytes 2211840 | tf_op jit(solution)/shard_map/all_gather | solution.py:246
  575.1 593.8 %all-gather.72.cloned.1.call-start = ((), (), s32[]{:S(2)}) async-start(), calls=%async_computation.20 | async-start | bytes 5898240 | tf_op jit(solution)/shard_map/all_gather | solution.py:248
  575.8 636.1 %all-gather.66.cloned.1.call-start = ((), (), s32[]{:S(2)}) async-start(), calls=%async_computation.17 | async-start | bytes 5898240 | tf_op jit(solution)/shard_map/all_gather | solution.py:247
  576.6 998.4 %all-reduce.14.cloned.1.call-start = ((), (), s32[]{:S(2)}) async-start(), calls=%async_computation.36 | async-start | bytes 20316160 | tf_op jit(solution)/shard_map/psum | solution.py:140
  1224.5 38.5 %copy-start.23 = (f32[128,960]{0,1:T(8,128)S(1)}, f32[128,960]{0,1:T(8,128)}, u32[]{:S(2)}) copy-start(f32[128,960]{0,1:T(8,128)} %get-tuple-element.46) | copy-start | bytes 1474564
  (81 other events, 349.2 us)
Sparse Core Ops, SparseCore 0:
  10.5 30.1 all-gather.81
  42.5 27.3 all-gather.83
  72.4 47.8 all-gather.85
  122.0 39.7 all-gather.87
  164.1 41.1 all-gather.89
  207.5 31.2 all-gather.91
  241.3 27.4 all-gather.93
  271.2 39.7 all-gather.97
  313.4 41.1 all-gather.99
  356.3 39.7 all-gather.95
  434.1 37.3 reduce-scatter.4
  475.2 37.3 reduce-scatter.6
  514.4 27.5 all-gather.51
  544.4 27.6 all-gather.53
  573.7 30.1 all-gather.61
  605.7 27.5 all-gather.59
  636.9 37.3 reduce-scatter.10
  678.0 37.3 reduce-scatter.8
  717.2 27.5 all-gather.47
  747.1 27.6 all-gather.49
  776.7 27.6 all-gather.55
  806.8 27.6 all-gather.57
  836.3 27.6 all-gather.77
  865.7 41.1 all-gather.75
  908.7 27.6 all-gather.101
  938.7 41.1 all-gather.79
  981.6 27.6 all-gather.67
  1011.7 41.1 all-gather.73
  1055.3 41.1 all-gather.69
  1098.2 27.6 all-gather.63
  1127.7 41.1 all-gather.71
  1170.7 41.1 all-gather.65
  1217.5 357.5 all-reduce.13
where the time goes:
time: 1600 us; the launch traced here: 1590 us
  waiting for transfers between devices  1100 us (69%)
  blocking collectives  205 us (13%)
  matrix products  191 us (12%)
  other arithmetic  38.1 us (2%)
  local copies, waits for them, and re-layouts  36.4 us (2%)
  between operations  17.4 us (1%)
    psum x1, waiting for transfers between devices, replica_total(): lax.psum((share_gain_attn, share_query, share_key, share_value, share_out...  311 us
    all_gather x2, waiting for transfers between devices, layer_backward(): piece_up = lax.all_gather(grad_up_low, 'group', axis=0, tiled=True)  86.6 us
    all_gather x2, waiting for transfers between devices, layer_backward(): piece_hidden = lax.all_gather(hidden, 'group', axis=0, tiled=True)  86.4 us
    all_gather x2, waiting for transfers between devices, on_device(): lax.all_gather(w_down[layer_index], 'group', axis=0, tiled=True)  78 us
    all_gather x2, waiting for transfers between devices, layer_backward(): piece_gate = lax.all_gather(grad_gate_low, 'group', axis=0, tiled=True)  77.5 us
    reduce_scatter x2, waiting for transfers between devices, layer_backward(): lax.psum_scatter(grad_value_all, 'group', scatter_dimension=0, tiled=True)  75.5 us
    reduce_scatter x2, waiting for transfers between devices, layer_backward(): lax.psum_scatter(grad_key_all, 'group', scatter_dimension=0, tiled=True)  65.6 us
    all_gather x2, waiting for transfers between devices, layer_backward(): piece_branch = lax.all_gather(branch_low, 'group', axis=0, tiled=True)  51.5 us
  transfers between devices with their start and end apart: 33, of which 27 were waited for; matrix products, arithmetic and copies ran while one was open for 13% of the time, Pallas kernels for 0%

commit v1 on v0

--- a/solution.py
+++ b/solution.py
@@ -9,6 +9,19 @@
 LAYERS = 2
 epsilon = 1e-05
 rope_base = 100000.0
+
+
+def ring_gather(x, axis, dim):
+    ways = lax.axis_size(axis)
+    up = [(d, (d + 1) % ways) for d in range(ways)]
+    down = [(d, (d - 1) % ways) for d in range(ways)]
+    earlier, later = ([x], [x])
+    for _ in range(ways // 2):
+        earlier.append(lax.ppermute(earlier[-1], axis, up))
+    for _ in range((ways - 1) // 2):
+        later.append(lax.ppermute(later[-1], axis, down))
+    line = jnp.concatenate([*earlier[::-1], *later[1:]], axis=dim)
+    return jnp.roll(line, (lax.axis_index(axis) - ways // 2) * x.shape[dim], axis=dim)
 
 
 def forward_dot(left, right):
@@ -245,7 +258,7 @@
     piece_after = lax.all_gather(after_low, "group", axis=0, tiled=True)
     piece_ffn = lax.all_gather(normed_ffn, "group", axis=0, tiled=True)
     piece_gate = lax.all_gather(grad_gate_low, "group", axis=0, tiled=True)
-    piece_up = lax.all_gather(grad_up_low, "group", axis=0, tiled=True)
+    piece_up = ring_gather(grad_up_low, "group", 0)
     piece_hidden = lax.all_gather(hidden, "group", axis=0, tiled=True)
     piece_branch = lax.all_gather(branch_low, "group", axis=0, tiled=True)
     left_attn = owned_columns(piece_attn, owner, members)

time: 1600 us -> 1540 us (0.963)
  waiting for transfers between devices: 1100 us -> 973 us
  blocking collectives: 205 us -> 238 us
  local copies, waits for them, and re-layouts: 36.4 us -> 60.6 us
  starting transfers between devices: 1.46 us -> 18 us
    all_gather x2 -> x0, waiting for transfers between devices: 86.6 us -> none  [layer_backward(): piece_up = lax.all_gather(grad_up_low, 'group', axis=0, tiled=True)]
    ppermute x0 -> x14, waiting for transfers between devices: none -> 50.2 us  [the longest x8 49.1 us: ring_gather(): earlier.append(lax.ppermute(earlier[-1], axis, up))]
    all_gather x2, waiting for transfers between devices: 49.9 us -> 11.3 us  [layer_backward(): piece_ffn = lax.all_gather(normed_ffn, 'group', axis=0, tiled=True)]
    all_gather x2, blocking collectives: 22.6 us -> 54.8 us  [layer_backward(): piece_key = lax.all_gather(key_back, 'group', axis=0, tiled=True)]
    reduce_scatter x2, waiting for transfers between devices: 75.5 us -> 50.2 us  [layer_backward(): lax.psum_scatter(grad_value_all, 'group', scatter_dimension=0, tiled=True)]
    all_gather x2, waiting for transfers between devices: 51.4 us -> 26.3 us  [layer_backward(): piece_mixed = lax.all_gather(mixed_heads, 'group', axis=0, tiled=True)]
    unnamed x207 -> x191, local copies, waits for them, and re-layouts: 12.1 us -> 31.1 us
    ppermute x0 -> x14, starting transfers between devices: none -> 16.3 us  [the longest x6 15.8 us: ring_gather(): later.append(lax.ppermute(later[-1], axis, down))]
  transfers between devices with their start and end apart: 33 -> 45, of which waited for: 27 -> 27; matrix products, arithmetic and copies ran while one was open for 13% -> 15% of each run, Pallas kernels for 0% -> 0%
where the time goes in v1:
time: 1540 us; the launch traced here: 1530 us
  waiting for transfers between devices  973 us (63%)
  blocking collectives  238 us (15%)
  matrix products  186 us (12%)
  local copies, waits for them, and re-layouts  60.6 us (4%)
  other arithmetic  38.5 us (2%)
  starting transfers between devices  18 us (1%)
  between operations  17.3 us (1%)
    psum x1, waiting for transfers between devices, replica_total(): lax.psum((share_gain_attn, share_query, share_key, share_value, share_out...  311 us
    all_gather x2, waiting for transfers between devices, layer_backward(): piece_hidden = lax.all_gather(hidden, 'group', axis=0, tiled=True)  86.5 us
    all_gather x2, waiting for transfers between devices, on_device(): lax.all_gather(w_down[layer_index], 'group', axis=0, tiled=True)  78.3 us
    all_gather x2, waiting for transfers between devices, layer_backward(): piece_gate = lax.all_gather(grad_gate_low, 'group', axis=0, tiled=True)  78.2 us
    reduce_scatter x2, waiting for transfers between devices, layer_backward(): lax.psum_scatter(grad_key_all, 'group', scatter_dimension=0, tiled=True)  65.2 us
    all_gather x2, blocking collectives, layer_backward(): piece_key = lax.all_gather(key_back, 'group', axis=0, tiled=True)  54.8 us
    dot_general x14, matrix products, over_rows(): lax.dot_general(left, right, (((0,), (0,)), ((), ())), preferred_element_...  51.6 us
    all_gather x2, waiting for transfers between devices, layer_backward(): piece_branch = lax.all_gather(branch_low, 'group', axis=0, tiled=True)  51.3 us
  transfers between devices with their start and end apart: 45, of which 27 were waited for; matrix products, arithmetic and copies ran while one was open for 15% of the time, Pallas kernels for 0%

profile of v1, /device:TPU:0, one launch (start us, length us, event | category | flops | bytes accessed | tf_op | source)
XLA Modules:
  0.0 1530.3 jit_solution(3843086062338573759)
XLA Ops:
  23.0 15.8 %all-reduce.11 = (bf16[960]{0:T(1024)(128)(2,1)S(1)}, bf16[960]{0:T(1024)(128)(2,1)S(1)}, bf16[960]{0:T(1024)(128)(2,1)S(1)}, bf16[960]{0:T(1024)(128)(2,1)S(1)}) all-reduce(bf16[960]{0:T(1024)(128)(2,1)S(1)} %dynamic-update-slice, bf16[960]{0:T(1024)(128)(2,1)S(1)} %dynamic-update-slice.1, ...), channel_id=2, replica_groups=mesh['group'=8,'replica'=4] {'group'}, use_global_device_ids=true, to_apply=%add | all-reduce | flops 3840 | bytes 15360
  39.2 12.0 all-gather.2
  54.5 9.2 all_gather.152
  65.0 15.3 all-gather.1
  83.0 11.6 all_gather.150
  94.8 20.0 %all-gather.11 = bf16[1,960,320]{2,0,1:T(2,128)(2,1)S(1)} all-gather(bf16[1,120,320]{2,0,1:T(2,128)(2,1)S(1)} %copy.82), channel_id=13, replica_groups=mesh['group'=8,'replica'=4] {'group'}, dimensions={1}, use_global_device_ids=true | all-gather | bytes 691200 | tf_op jit(solution)/shard_map/all_gather | solution.py:319
  118.3 12.8 all-gather.10
  138.6 5.7 fusion.250
  154.7 6.4 all-gather.82.cloned.1.call-done
  165.5 39.0 %all-gather.84.cloned.1.call-done = bf16[1,2560,960]{2,1,0:T(8,128)(2,1)} async-done(((bf16[1,320,960]{2,1,0:T(8,128)(2,1)}), bf16[1,2560,960]{2,1,0:T(8,128)(2,1)}) %all-gather.84.cloned.1.call-update) | async-done | bytes 4915216 | tf_op jit(solution)/shard_map/all_gather | solution.py:325
  210.6 11.9 all_gather.163
  222.9 13.0 all_gather.161
  240.9 6.7 fusion.255
  251.8 15.7 %all-gather.88.cloned.1.call-done = bf16[1,960,960]{2,1,0:T(8,128)(2,1)} async-done(((bf16[1,120,960]{2,1,0:T(8,128)(2,1)}), bf16[1,960,960]{2,1,0:T(8,128)(2,1)}) %all-gather.88.cloned.1.call-update) | async-done | bytes 1843216 | tf_op jit(solution)/shard_map/all_gather | solution.py:321
  270.2 39.5 %all-gather.92.cloned.1.call-done = bf16[1,960,2560]{2,1,0:T(8,128)(2,1)} async-done(((bf16[1,120,2560]{2,1,0:T(8,128)(2,1)}), bf16[1,960,2560]{2,1,0:T(8,128)(2,1)}) %all-gather.92.cloned.1.call-update) | async-done | bytes 4915216 | tf_op jit(solution)/shard_map/all_gather | solution.py:324
  314.1 39.3 %all-gather.94.cloned.1.call-done = bf16[1,2560,960]{2,1,0:T(8,128)(2,1)} async-done(((bf16[1,320,960]{2,1,0:T(8,128)(2,1)}), bf16[1,2560,960]{2,1,0:T(8,128)(2,1)}) %all-gather.94.cloned.1.call-update) | async-done | bytes 4915216 | tf_op jit(solution)/shard_map/all_gather | solution.py:325
  358.8 36.1 %all-gather.90.cloned.1.call-done = bf16[1,960,2560]{2,1,0:T(8,128)(2,1)} async-done(((bf16[1,120,2560]{2,1,0:T(8,128)(2,1)}), bf16[1,960,2560]{2,1,0:T(8,128)(2,1)}) %all-gather.90.cloned.1.call-update) | async-done | bytes 4915216 | tf_op jit(solution)/shard_map/all_gather | solution.py:323
  413.8 8.1 fusion.5
  421.9 6.8 fusion.7
  445.5 25.0 %reduce-scatter.5.cloned.1.call-done = f32[128,5,64]{0,2,1:T(8,128)} async-done(((f32[1024,5,64]{0,2,1:T(8,128)}), f32[128,5,64]{0,2,1:T(8,128)}) %reduce-scatter.5.cloned.1.call-update) | async-done | bytes 163856 | tf_op jit(solution)/shard_map/reduce_scatter | solution.py:233
  472.7 38.8 %reduce-scatter.7.cloned.1.call-done = f32[128,5,64]{0,2,1:T(8,128)} async-done(((f32[1024,5,64]{0,2,1:T(8,128)}), f32[128,5,64]{0,2,1:T(8,128)}) %reduce-scatter.7.cloned.1.call-update) | async-done | bytes 163856 | tf_op jit(solution)/shard_map/reduce_scatter | solution.py:234
  518.4 5.8 multiply_convert_fusion.1
  540.3 7.7 fusion.2
  548.0 7.1 fusion.4
  569.8 10.9 collective-permute-done.7
  583.3 21.0 %collective-permute-done.8 = bf16[128,2560]{1,0:T(8,128)(2,1)S(1)} collective-permute-done((bf16[128,2560]{1,0:T(8,128)(2,1)S(1)}, bf16[128,2560]{1,0:T(8,128)(2,1)S(1)}, u32[]{:S(2)}, u32[]{:S(2)}) %collective-permute-start.8) | collective-permute-done | bytes 655392 | tf_op jit(solution)/shard_map/ppermute | solution.py:20
  609.6 14.0 collective-permute-done.9
  627.8 36.2 %all_gather.175 = bf16[1024,320]{0,1:T(8,128)(2,1)} all-gather(bf16[128,320]{0,1:T(8,128)(2,1)S(1)} %bitcast.438), channel_id=1, replica_groups=mesh['group'=8,'replica'=4] {'group'}, dimensions={0}, use_global_device_ids=true | all-gather | bytes 737280 | tf_op jit(solution)/shard_map/all_gather | solution.py:255
  664.1 12.0 all_gather.177
  706.8 6.3 fusion.50
  713.1 11.4 reduce-scatter.11.cloned.1.call-done
  725.4 40.2 %reduce-scatter.9.cloned.1.call-done = f32[128,5,64]{0,2,1:T(8,128)} async-done(((f32[1024,5,64]{0,2,1:T(8,128)}), f32[128,5,64]{0,2,1:T(8,128)}) %reduce-scatter.9.cloned.1.call-update) | async-done | bytes 163856 | tf_op jit(solution)/shard_map/reduce_scatter | solution.py:233
  766.7 18.6 %all_gather.174 = bf16[1024,320]{0,1:T(8,128)(2,1)} all-gather(bf16[128,320]{0,1:T(8,128)(2,1)S(1)} %bitcast.439), channel_id=1, replica_groups=mesh['group'=8,'replica'=4] {'group'}, dimensions={0}, use_global_device_ids=true | all-gather | bytes 737280 | tf_op jit(solution)/shard_map/all_gather | solution.py:255
  785.3 12.8 all_gather.176
  817.2 11.3 all-gather.62.cloned.1.call-done
  828.5 6.3 fusion.53
  834.7 23.3 %all-gather.48.cloned.1.call-done = bf16[1024,960]{0,1:T(8,128)(2,1)} async-done(((bf16[128,960]{0,1:T(8,128)(2,1)}), bf16[1024,960]{0,1:T(8,128)(2,1)}) %all-gather.48.cloned.1.call-update) | async-done | bytes 1966096 | tf_op jit(solution)/shard_map/all_gather | solution.py:254
  861.3 26.3 %all-gather.54.cloned.1.call-done = bf16[1024,960]{0,1:T(8,128)(2,1)} async-done(((bf16[128,960]{0,1:T(8,128)(2,1)}), bf16[1024,960]{0,1:T(8,128)(2,1)}) %all-gather.54.cloned.1.call-update) | async-done | bytes 1966096 | tf_op jit(solution)/shard_map/all_gather | solution.py:257
  887.5 29.4 %all-gather.56.cloned.1.call-done = bf16[1024,960]{0,1:T(8,128)(2,1)} async-done(((bf16[128,960]{0,1:T(8,128)(2,1)}), bf16[1024,960]{0,1:T(8,128)(2,1)}) %all-gather.56.cloned.1.call-update) | async-done | bytes 1966096 | tf_op jit(solution)/shard_map/all_gather | solution.py:258
  920.2 26.3 %all-gather.72.cloned.1.call-done = bf16[1024,960]{0,1:T(8,128)(2,1)} async-done(((bf16[128,960]{0,1:T(8,128)(2,1)}), bf16[1024,960]{0,1:T(8,128)(2,1)}) %all-gather.72.cloned.1.call-update) | async-done | bytes 1966096 | tf_op jit(solution)/shard_map/all_gather | solution.py:263
  946.5 42.9 %all-gather.70.cloned.1.call-done = bf16[1024,2560]{1,0:T(8,128)(2,1)} async-done(((bf16[128,2560]{1,0:T(8,128)(2,1)}), bf16[1024,2560]{1,0:T(8,128)(2,1)}) %all-gather.70.cloned.1.call-update) | async-done | bytes 5242896 | tf_op jit(solution)/shard_map/all_gather | solution.py:262
  993.7 25.1 %all-gather.96.cloned.1.call-done = bf16[1,1024,960]{1,2,0:T(8,128)(2,1)} async-done(((bf16[1,128,960]{1,2,0:T(8,128)(2,1)}), bf16[1,1024,960]{1,2,0:T(8,128)(2,1)}) %all-gather.96.cloned.1.call-update) | async-done | bytes 1966096 | tf_op jit(solution)/shard_map/all_gather | solution.py:263
  1018.7 43.6 %all-gather.74.cloned.1.call-done = bf16[1024,2560]{1,0:T(8,128)(2,1)} async-done(((bf16[128,2560]{1,0:T(8,128)(2,1)}), bf16[1024,2560]{1,0:T(8,128)(2,1)}) %all-gather.74.cloned.1.call-update) | async-done | bytes 5242896 | tf_op jit(solution)/shard_map/all_gather | solution.py:262
  1066.6 39.3 %all-gather.68.cloned.1.call-done = bf16[1024,2560]{1,0:T(8,128)(2,1)} async-done(((bf16[128,2560]{1,0:T(8,128)(2,1)}), bf16[1024,2560]{1,0:T(8,128)(2,1)}) %all-gather.68.cloned.1.call-update) | async-done | bytes 5242896 | tf_op jit(solution)/shard_map/all_gather | solution.py:260
  1110.5 38.9 %all-gather.64.cloned.1.call-done = bf16[1024,2560]{1,0:T(8,128)(2,1)} async-done(((bf16[128,2560]{1,0:T(8,128)(2,1)}), bf16[1024,2560]{1,0:T(8,128)(2,1)}) %all-gather.64.cloned.1.call-update) | async-done | bytes 5242896 | tf_op jit(solution)/shard_map/all_gather | solution.py:260
  1162.3 24.9 %all-reduce.8 = (f32[960]{0:T(1024)S(1)}, f32[960]{0:T(1024)S(1)}, f32[960]{0:T(1024)S(1)}, f32[960]{0:T(1024)S(1)}) all-reduce(f32[960]{0:T(1024)S(1)} %copy-done.64, f32[960]{0:T(1024)S(1)} %get-tuple-element.18, f32[960]{0:T(1024)S(1)} %copy-done.63, ...), channel_id=26, replica_groups=mesh['group'=8,'replica'=4] {'group'}, use_global_device_ids=true, to_apply=%region_22.23.clone | all-reduce | flops 3840 | bytes 30720
  1187.5 11.7 all-reduce.9
  1201.3 311.5 %all-reduce.14.cloned.1.call-done = (f32[1,120,960]{2,1,0:T(8,128)}, f32[1,120,960]{2,1,0:T(8,128)}, f32[1,120,320]{1,2,0:T(8,128)}, f32[1,120,320]{1,2,0:T(8,12...) async-done(((f32[1,120,960]{2,1,0:T(8,128)}, ...) | async-done | bytes 9830416 | tf_op jit(solution)/shard_map/psum | solution.py:153
  (406 shorter events, 259.6 us)
Async XLA Ops:
  7.2 127.6 %all-gather.76.cloned.1.call-start = ((), (), s32[]{:S(2)}) async-start(), calls=%async_computation.23 | async-start | bytes 2211840 | tf_op jit(solution)/shard_map/all_gather | solution.py:318
  9.1 139.4 %all-gather.78.cloned.1.call-start = ((), (), s32[]{:S(2)}) async-start(), calls=%async_computation.24 | async-start | bytes 2211840 | tf_op jit(solution)/shard_map/all_gather | solution.py:321
  11.1 140.2 %all-gather.80.cloned.1.call-start = ((), (), s32[]{:S(2)}) async-start(), calls=%async_computation.25 | async-start | bytes 5529600 | tf_op jit(solution)/shard_map/all_gather | solution.py:323
  13.6 147.5 %all-gather.82.cloned.1.call-start = ((), (), s32[]{:S(2)}) async-start(), calls=%async_computation.26 | async-start | bytes 5529600 | tf_op jit(solution)/shard_map/all_gather | solution.py:324
  16.1 188.4 %all-gather.84.cloned.1.call-start = ((), (), s32[]{:S(2)}) async-start(), calls=%async_computation.27 | async-start | bytes 5898240 | tf_op jit(solution)/shard_map/all_gather | solution.py:325
  17.4 220.3 %all-gather.86.cloned.1.call-start = ((), (), s32[]{:S(2)}) async-start(), calls=%async_computation.28 | async-start | bytes 2211840 | tf_op jit(solution)/shard_map/all_gather | solution.py:318
  18.0 249.5 %all-gather.88.cloned.1.call-start = ((), (), s32[]{:S(2)}) async-start(), calls=%async_computation.29 | async-start | bytes 2211840 | tf_op jit(solution)/shard_map/all_gather | solution.py:321
  18.7 291.0 %all-gather.92.cloned.1.call-start = ((), (), s32[]{:S(2)}) async-start(), calls=%async_computation.31 | async-start | bytes 5529600 | tf_op jit(solution)/shard_map/all_gather | solution.py:324
  19.5 333.9 %all-gather.94.cloned.1.call-start = ((), (), s32[]{:S(2)}) async-start(), calls=%async_computation.32 | async-start | bytes 5898240 | tf_op jit(solution)/shard_map/all_gather | solution.py:325
  20.2 374.7 %all-gather.90.cloned.1.call-start = ((), (), s32[]{:S(2)}) async-start(), calls=%async_computation.30 | async-start | bytes 5529600 | tf_op jit(solution)/shard_map/all_gather | solution.py:323
  20.8 449.8 %reduce-scatter.5.cloned.1.call-start = ((), (), s32[]{:S(2)}) async-start(), calls=%async_computation.4 | async-start | bytes 1474560 | tf_op jit(solution)/shard_map/reduce_scatter | solution.py:233
  39.0 98.6 %copy-start.65 = (f32[128]{0:T(128)}, f32[128]{0:T(128)S(1)}, u32[]{:S(2)}) copy-start(f32[128]{0:T(128)S(1)} %add_rsqrt_fusion.3) | copy-start | bytes 1540
  270.0 140.5 %copy-start.69 = (f32[128]{0:T(128)}, f32[128]{0:T(128)S(1)}, u32[]{:S(2)}) copy-start(f32[128]{0:T(128)S(1)} %add_rsqrt_fusion) | copy-start | bytes 1540
  270.2 88.6 %copy-start.28 = (bf16[128,960]{0,1:T(8,128)(2,1)}, bf16[128,960]{0,1:T(8,128)(2,1)S(1)}, u32[]{:S(2)}) copy-start(bf16[128,960]{0,1:T(8,128)(2,1)S(1)} %multiply_convert_fusion.6) | copy-start | bytes 737284
  433.1 78.5 %reduce-scatter.7.cloned.1.call-start = ((), (), s32[]{:S(2)}) async-start(), calls=%async_computation.5 | async-start | bytes 1474560 | tf_op jit(solution)/shard_map/reduce_scatter | solution.py:234
  438.8 257.3 %all-gather.50.cloned.1.call-start = ((), (), s32[]{:S(2)}) async-start(), calls=%async_computation.10 | async-start | bytes 2211840 | tf_op jit(solution)/shard_map/all_gather | solution.py:253
  439.6 258.7 %all-gather.52.cloned.1.call-start = ((), (), s32[]{:S(2)}) async-start(), calls=%async_computation.11 | async-start | bytes 2211840 | tf_op jit(solution)/shard_map/all_gather | solution.py:254
  443.7 257.8 %all-gather.60.cloned.1.call-start = ((), (), s32[]{:S(2)}) async-start(), calls=%async_computation.15 | async-start | bytes 2211840 | tf_op jit(solution)/shard_map/all_gather | solution.py:258
  444.3 257.2 %all-gather.58.cloned.1.call-start = ((), (), s32[]{:S(2)}) async-start(), calls=%async_computation.14 | async-start | bytes 2211840 | tf_op jit(solution)/shard_map/all_gather | solution.py:257
  444.9 261.9 %all-gather.66.cloned.1.call-start = ((), (), s32[]{:S(2)}) async-start(), calls=%async_computation.18 | async-start | bytes 2211840 | tf_op jit(solution)/shard_map/all_gather | solution.py:259
  445.5 278.9 %reduce-scatter.11.cloned.1.call-start = ((), (), s32[]{:S(2)}) async-start(), calls=%async_computation.7 | async-start | bytes 1474560 | tf_op jit(solution)/shard_map/reduce_scatter | solution.py:234
  539.8 225.9 %reduce-scatter.9.cloned.1.call-start = ((), (), s32[]{:S(2)}) async-start(), calls=%async_computation.6 | async-start | bytes 1474560 | tf_op jit(solution)/shard_map/reduce_scatter | solution.py:233
  559.5 238.6 %all-gather.46.cloned.1.call-start = ((), (), s32[]{:S(2)}) async-start(), calls=%async_computation.8 | async-start | bytes 2211840 | tf_op jit(solution)/shard_map/all_gather | solution.py:253
  560.1 268.4 %all-gather.62.cloned.1.call-start = ((), (), s32[]{:S(2)}) async-start(), calls=%async_computation.16 | async-start | bytes 2211840 | tf_op jit(solution)/shard_map/all_gather | solution.py:259
  560.8 297.2 %all-gather.48.cloned.1.call-start = ((), (), s32[]{:S(2)}) async-start(), calls=%async_computation.9 | async-start | bytes 2211840 | tf_op jit(solution)/shard_map/all_gather | solution.py:254
  564.9 322.6 %all-gather.54.cloned.1.call-start = ((), (), s32[]{:S(2)}) async-start(), calls=%async_computation.12 | async-start | bytes 2211840 | tf_op jit(solution)/shard_map/all_gather | solution.py:257
  565.7 351.2 %all-gather.56.cloned.1.call-start = ((), (), s32[]{:S(2)}) async-start(), calls=%async_computation.13 | async-start | bytes 2211840 | tf_op jit(solution)/shard_map/all_gather | solution.py:258
  566.3 380.2 %all-gather.72.cloned.1.call-start = ((), (), s32[]{:S(2)}) async-start(), calls=%async_computation.21 | async-start | bytes 2211840 | tf_op jit(solution)/shard_map/all_gather | solution.py:263
  567.0 422.3 %all-gather.70.cloned.1.call-start = ((), (), s32[]{:S(2)}) async-start(), calls=%async_computation.20 | async-start | bytes 5898240 | tf_op jit(solution)/shard_map/all_gather | solution.py:262
  567.6 451.1 %all-gather.96.cloned.1.call-start = ((), (), s32[]{:S(2)}) async-start(), calls=%async_computation.33 | async-start | bytes 2211840 | tf_op jit(solution)/shard_map/all_gather | solution.py:263
  568.2 494.2 %all-gather.74.cloned.1.call-start = ((), (), s32[]{:S(2)}) async-start(), calls=%async_computation.22 | async-start | bytes 5898240 | tf_op jit(solution)/shard_map/all_gather | solution.py:262
  568.9 537.0 %all-gather.68.cloned.1.call-start = ((), (), s32[]{:S(2)}) async-start(), calls=%async_computation.19 | async-start | bytes 5898240 | tf_op jit(solution)/shard_map/all_gather | solution.py:260
  569.7 579.7 %all-gather.64.cloned.1.call-start = ((), (), s32[]{:S(2)}) async-start(), calls=%async_computation.17 | async-start | bytes 5898240 | tf_op jit(solution)/shard_map/all_gather | solution.py:260
  569.7 11.0 collective-permute-start.7
  580.7 23.6 %collective-permute-start.8 = (bf16[128,2560]{1,0:T(8,128)(2,1)S(1)}, bf16[128,2560]{1,0:T(8,128)(2,1)S(1)}, u32[]{:S(2)}, u32[]{:S(2)}) collective-permute-start(bf16[128,2560]{1,0:T(8,128)(2,1)S(1)} %collective-permute-done.7), channel_id=1, source_target_pairs={{0,4},{4,8},{8,12},{12,16},{16,20},{20,24},{24,28},{28,0},{1,5},{5... | collective-permute-start | bytes 1966088 | tf_op jit(solution)/shard_map/ppermute | solution.py:20
  580.7 23.6 %collective-permute-start.11 = (bf16[128,2560]{1,0:T(8,128)(2,1)S(1)}, bf16[128,2560]{1,0:T(8,128)(2,1)S(1)}, u32[]{:S(2)}, u32[]{:S(2)}) collective-permute-start(bf16[128,2560]{1,0:T(8,128)(2,1)S(1)} %copy-done.22), channel_id=1, source_target_pairs={{0,28},{4,0},{8,4},{12,8},{16,12},{20,16},{24,20},{28,24},{1,29},{... | collective-permute-start | bytes 1966088 | tf_op jit(solution)/shard_map/ppermute | solution.py:22
  604.3 19.4 %collective-permute-start.9 = (bf16[128,2560]{1,0:T(8,128)(2,1)S(1)}, bf16[128,2560]{1,0:T(8,128)(2,1)}, u32[]{:S(2)}, u32[]{:S(2)}) collective-permute-start(bf16[128,2560]{1,0:T(8,128)(2,1)S(1)} %collective-permute-done.8), channel_id=1, source_target_pairs={{0,4},{4,8},{8,12},{12,16},{16,20},{20,24},{24,28},{28,0},{1,5},{5... | collective-permute-start | bytes 1966088 | tf_op jit(solution)/shard_map/ppermute | solution.py:20
  604.3 20.5 %collective-permute-start.12 = (bf16[128,2560]{1,0:T(8,128)(2,1)S(1)}, bf16[128,2560]{1,0:T(8,128)(2,1)}, u32[]{:S(2)}, u32[]{:S(2)}) collective-permute-start(bf16[128,2560]{1,0:T(8,128)(2,1)S(1)} %collective-permute-done.11), channel_id=1, source_target_pairs={{0,28},{4,0},{8,4},{12,8},{16,12},{20,16},{24,20},{28,24},{1,29},{... | collective-permute-start | bytes 1966088 | tf_op jit(solution)/shard_map/ppermute | solution.py:22
  607.0 69.1 %collective-permute-start = (bf16[128,2560]{1,0:T(8,128)(2,1)}, bf16[128,2560]{1,0:T(8,128)(2,1)}, u32[]{:S(2)}, u32[]{:S(2)}) collective-permute-start(bf16[128,2560]{1,0:T(8,128)(2,1)} %copy-done.23), channel_id=1, source_target_pairs={{0,4},{4,8},{8,12},{12,16},{16,20},{20,24},{24,28},{28,0},{1,5},{5... | collective-permute-start | bytes 1966088 | tf_op jit(solution)/shard_map/ppermute | solution.py:20
  607.0 69.4 %collective-permute-start.4 = (bf16[128,2560]{1,0:T(8,128)(2,1)}, bf16[128,2560]{1,0:T(8,128)(2,1)}, u32[]{:S(2)}, u32[]{:S(2)}) collective-permute-start(bf16[128,2560]{1,0:T(8,128)(2,1)} %copy-done.23), channel_id=1, source_target_pairs={{0,28},{4,0},{8,4},{12,8},{16,12},{20,16},{24,20},{28,24},{1,29},{... | collective-permute-start | bytes 1966088 | tf_op jit(solution)/shard_map/ppermute | solution.py:22
  623.6 55.0 %collective-permute-start.10 = (bf16[128,2560]{1,0:T(8,128)(2,1)}, bf16[128,2560]{1,0:T(8,128)(2,1)}, u32[]{:S(2)}, u32[]{:S(2)}) collective-permute-start(bf16[128,2560]{1,0:T(8,128)(2,1)} %collective-permute-done.9), channel_id=1, source_target_pairs={{0,4},{4,8},{8,12},{12,16},{16,20},{20,24},{24,28},{28,0},{1,5},{5... | collective-permute-start | bytes 1966088 | tf_op jit(solution)/shard_map/ppermute | solution.py:20
  624.8 63.5 %collective-permute-start.13 = (bf16[128,2560]{1,0:T(8,128)(2,1)}, bf16[128,2560]{1,0:T(8,128)(2,1)}, u32[]{:S(2)}, u32[]{:S(2)}) collective-permute-start(bf16[128,2560]{1,0:T(8,128)(2,1)} %collective-permute-done.12), channel_id=1, source_target_pairs={{0,28},{4,0},{8,4},{12,8},{16,12},{20,16},{24,20},{28,24},{1,29},{... | collective-permute-start | bytes 1966088 | tf_op jit(solution)/shard_map/ppermute | solution.py:22
  627.7 885.0 %all-reduce.14.cloned.1.call-start = ((), (), s32[]{:S(2)}) async-start(), calls=%async_computation.34 | async-start | bytes 20316160 | tf_op jit(solution)/shard_map/psum | solution.py:153
  676.0 17.4 %collective-permute-start.1 = (bf16[128,2560]{1,0:T(8,128)(2,1)}, bf16[128,2560]{1,0:T(8,128)(2,1)}, u32[]{:S(2)}, u32[]{:S(2)}) collective-permute-start(bf16[128,2560]{1,0:T(8,128)(2,1)} %collective-permute-done), channel_id=1, source_target_pairs={{0,4},{4,8},{8,12},{12,16},{16,20},{20,24},{24,28},{28,0},{1,5},{5... | collective-permute-start | bytes 1966088 | tf_op jit(solution)/shard_map/ppermute | solution.py:20
  676.4 17.0 %collective-permute-start.5 = (bf16[128,2560]{1,0:T(8,128)(2,1)}, bf16[128,2560]{1,0:T(8,128)(2,1)}, u32[]{:S(2)}, u32[]{:S(2)}) collective-permute-start(bf16[128,2560]{1,0:T(8,128)(2,1)} %collective-permute-done.4), channel_id=1, source_target_pairs={{0,28},{4,0},{8,4},{12,8},{16,12},{20,16},{24,20},{28,24},{1,29},{... | collective-permute-start | bytes 1966088 | tf_op jit(solution)/shard_map/ppermute | solution.py:22
  693.4 73.1 %collective-permute-start.2 = (bf16[128,2560]{1,0:T(8,128)(2,1)}, bf16[128,2560]{1,0:T(8,128)(2,1)}, u32[]{:S(2)}, u32[]{:S(2)}) collective-permute-start(bf16[128,2560]{1,0:T(8,128)(2,1)} %collective-permute-done.1), channel_id=1, source_target_pairs={{0,4},{4,8},{8,12},{12,16},{16,20},{20,24},{24,28},{28,0},{1,5},{5... | collective-permute-start | bytes 1966088 | tf_op jit(solution)/shard_map/ppermute | solution.py:20
  693.4 121.7 %collective-permute-start.6 = (bf16[128,2560]{1,0:T(8,128)(2,1)}, bf16[128,2560]{1,0:T(8,128)(2,1)}, u32[]{:S(2)}, u32[]{:S(2)}) collective-permute-start(bf16[128,2560]{1,0:T(8,128)(2,1)} %collective-permute-done.5), channel_id=1, source_target_pairs={{0,28},{4,0},{8,4},{12,8},{16,12},{20,16},{24,20},{28,24},{1,29},{... | collective-permute-start | bytes 1966088 | tf_op jit(solution)/shard_map/ppermute | solution.py:22
  766.6 35.7 %collective-permute-start.3 = (bf16[128,2560]{1,0:T(8,128)(2,1)}, bf16[128,2560]{1,0:T(8,128)(2,1)}, u32[]{:S(2)}, u32[]{:S(2)}) collective-permute-start(bf16[128,2560]{1,0:T(8,128)(2,1)} %collective-permute-done.2), channel_id=1, source_target_pairs={{0,4},{4,8},{8,12},{12,16},{16,20},{20,24},{24,28},{28,0},{1,5},{5... | collective-permute-start | bytes 1966088 | tf_op jit(solution)/shard_map/ppermute | solution.py:20
  (78 other events, 1158.8 us)
Sparse Core Ops, SparseCore 0:
  10.5 30.2 all-gather.75
  42.6 27.3 all-gather.77
  72.5 46.5 all-gather.79
  121.3 39.7 all-gather.81
  163.4 41.1 all-gather.83
  206.9 30.7 all-gather.85
  240.1 27.3 all-gather.87
  270.0 39.7 all-gather.91
  312.2 41.1 all-gather.93
  355.1 39.7 all-gather.89
  433.2 37.3 reduce-scatter.4
  474.2 37.3 reduce-scatter.6
  513.4 27.5 all-gather.49
  543.4 27.8 all-gather.51
  573.0 34.0 all-gather.59
  608.8 36.4 all-gather.57
  647.5 31.3 all-gather.65
  682.6 41.8 reduce-scatter.10
  728.3 37.3 reduce-scatter.8
  767.3 30.6 all-gather.45
  800.0 28.4 all-gather.61
  830.4 27.6 all-gather.47
  859.9 27.6 all-gather.53
  889.3 27.6 all-gather.55
  918.8 27.6 all-gather.71
  948.2 41.1 all-gather.69
  991.1 27.6 all-gather.95
  1021.2 41.1 all-gather.73
  1064.8 41.1 all-gather.67
  1108.2 41.1 all-gather.63
  1155.1 357.5 all-reduce.13
